TPU v7x, 32 devices: a whole 2x2x4 slice. The times are simulated.
32 devices in a mesh: stream: 2 (over x), span: 4 (over y, core), depth: 4 (over z).
Axes of the slice: x: 2, y: 2, z: 4, core: 2. Of those that a mesh axis runs over, the one named last changes fastest.
Arguments:
- forward_velocity: float32 [3, 16, 64, 512], P(None, 'stream', 'span', 'depth'), may hold values from -40 to 40, as said below
- adjoint_velocity: float32 [3, 16, 64, 512], P(None, 'stream', 'span', 'depth'), may hold values from -40 to 40, as said below
- weights: float32 [32, 81], replicated, may hold values from -0.625 to 0.625
Outputs:
- basis: float32 [32, 16, 64, 512], P(None, 'stream', 'span', 'depth')
Inputs may be any that keep to these rules, and one draw needn't show every extreme that they name: `forward_velocity`: a velocity field whose amplitude varies from cell to cell. `adjoint_velocity`: a velocity field whose amplitude varies from cell to cell.
All inputs are finite; a program needn't handle non-finite values.
Results may differ from a plain program's by a relative error of at most 0.0003.
Values sent between devices are 32-bit elements; how exact they have to be, the bound alone decides.
A program may use at most 64 MiB of HBM per device.

v0:
```python
import jax
import jax.numpy as jnp
from jax import lax
from jax.sharding import PartitionSpec as P


def padded_2(shard, sides, width):
    for axis, dim in sides:
        size, length = (lax.axis_size(axis), shard.shape[dim])
        up = [(i, (i + 1) % size) for i in range(size)]
        down = [(j, i) for i, j in up]
        last = lax.slice_in_dim(shard, length - width, length, axis=dim)
        initial = lax.slice_in_dim(shard, 0, width, axis=dim)
        before = lax.ppermute(last, axis, up)
        after = lax.ppermute(initial, axis, down)
        shard = jnp.concatenate([before, shard, after], axis=dim)
    return shard


def partner_2(value, axis, stride):
    mask = 2**stride
    pairs = [(source, source ^ mask) for source in range(lax.axis_size(axis))]
    return lax.ppermute(value, axis, pairs)


def along_axis(field, axis, offset):
    parts = [slice(None), slice(None), slice(None), slice(None)]
    length = field.shape[axis]
    parts[axis] = slice(2 + offset, length - 2 + offset)
    return field[tuple(parts)]


def slope_along(padded, axis):
    near = along_axis(padded, axis, 1) - along_axis(padded, axis, -1)
    far = along_axis(padded, axis, 2) - along_axis(padded, axis, -2)
    return (8.0 * near - far) / 12.0


def snapshots(piece_x, piece_y, piece_z, weights):
    slopes = [slope_along(piece_x, 1), slope_along(piece_y, 2), slope_along(piece_z, 3)]
    stacked = jnp.stack(slopes, axis=1)
    grads = stacked.reshape(stacked.shape[0] * 3, -1)
    products = (grads[:9][:, None, :] * grads[9:][None, :, :]).reshape(81, -1)
    return jnp.dot(
        weights, products, precision=lax.Precision.HIGHEST, preferred_element_type=jnp.float32
    )


def inner(left, right):
    return jnp.dot(left, right, precision=lax.Precision.HIGHEST, preferred_element_type=jnp.float32)


def upper_factor(matrix):
    return jnp.linalg.cholesky(matrix).T


def body(forward_velocity, adjoint_velocity, weights):
    stacked = jnp.concatenate([forward_velocity, adjoint_velocity], 0)
    padded = padded_2(stacked, (("stream", 1), ("span", 2), ("depth", 3)), 2)
    padded_x = padded[:, :, 2:-2, 2:-2]
    padded_y = padded[:, 2:-2, :, 2:-2]
    padded_z = padded[:, 2:-2, 2:-2, :]
    planes, rows_y, rows_z = (
        forward_velocity.shape[1],
        forward_velocity.shape[2],
        forward_velocity.shape[3],
    )
    count_snap = weights.shape[0]
    step_planes = 2
    block_cells = step_planes * rows_y * rows_z

    def block_step(index, carry):
        snaps, gram = carry
        start = index * step_planes
        piece_x = lax.dynamic_slice_in_dim(padded_x, start, step_planes + 4, 1)
        piece_y = lax.dynamic_slice_in_dim(padded_y, start, step_planes, 1)
        piece_z = lax.dynamic_slice_in_dim(padded_z, start, step_planes, 1)
        block = snapshots(piece_x, piece_y, piece_z, weights)
        snaps = lax.dynamic_update_slice_in_dim(snaps, block, index * block_cells, 1)
        return (snaps, gram + inner(block, block.T))

    snaps = jnp.zeros((count_snap, planes * rows_y * rows_z), jnp.float32)
    gram = jnp.zeros((count_snap, count_snap), jnp.float32)
    snaps, gram = lax.fori_loop(0, planes // step_planes, block_step, (snaps, gram))
    devices_all = lax.axis_size("stream") * lax.axis_size("span") * lax.axis_size("depth")
    cells = planes * rows_y * rows_z * devices_all
    factor = upper_factor(gram)
    for bit in range(lax.axis_size(("stream", "span", "depth")).bit_length() - 1):
        partner = partner_2(factor, ("stream", "span", "depth"), bit)
        factor = upper_factor(inner(factor.T, factor) + inner(partner.T, partner))
    total = inner(factor.T, factor)
    lower = jnp.linalg.cholesky(total / cells)
    inverse = jax.scipy.linalg.solve_triangular(
        lower, jnp.eye(count_snap, dtype=jnp.float32), lower=True
    )
    basis = inner(inverse, snaps)
    return basis.reshape(count_snap, planes, rows_y, rows_z)


def solution(mesh):
    in_specs = (P(None, "stream", "span", "depth"), P(None, "stream", "span", "depth"), P())
    out_specs = P(None, "stream", "span", "depth")
    return jax.shard_map(body, mesh=mesh, in_specs=in_specs, out_specs=out_specs, check_vma=False)
```

profile of v0, /device:TPU:0, one launch (start us, length us, event | category | flops | bytes accessed | tf_op | source)
XLA Modules:
  0.0 114.9 jit_solution(14848151590109033303)
XLA Ops:
  0.0 0.9 constant_dynamic-update-slice_fusion.1
  0.9 0.9 constant_dynamic-update-slice_fusion
  1.9 3.0 %collective-permute-start = (f32[6,2,16,128]{3,2,1,0:T(8,128)S(1)}, f32[6,2,16,128]{3,2,1,0:T(8,128)S(1)}, u32[]{:S(2)}, u32[]{:S(2)}) collective-permute-start(f32[6,2,16,128]{3,2,1,0:T(8,128)S(1)} %get-tuple-element.188), channel_id=1, source_target_pairs={{0,16},{16,0},{1,17},{17,1},{2,18},{18,2},{3,19},{19,3},{4,20},{20... | collective-permute-start | bytes 294920 | tf_op jit(solution)/shard_map/ppermute | solution.py:14
  5.0 3.4 %collective-permute-done = f32[6,2,16,128]{3,2,1,0:T(8,128)S(1)} collective-permute-done((f32[6,2,16,128]{3,2,1,0:T(8,128)S(1)}, f32[6,2,16,128]{3,2,1,0:T(8,128)S(1)}, u32[]{:S(2)}, u32[]{:S(2)}) %collective-permute-start) | collective-permute-done | bytes 98336 | tf_op jit(solution)/shard_map/ppermute | solution.py:14
  8.4 1.4 %collective-permute-done.1 = f32[6,2,16,128]{3,2,1,0:T(8,128)S(1)} collective-permute-done((f32[6,2,16,128]{3,2,1,0:T(8,128)S(1)}, f32[6,2,16,128]{3,2,1,0:T(8,128)S(1)}, u32[]{:S(2)}, u32[]{:S(2)}) %collective-permute-start.1) | collective-permute-done | bytes 98336 | tf_op jit(solution)/shard_map/ppermute | solution.py:15
  10.0 1.7 %collective-permute-start.3 = (f32[6,12,2,128]{3,2,1,0:T(2,128)S(1)}, f32[6,12,2,128]{3,2,1,0:T(2,128)S(1)}, u32[]{:S(2)}, u32[]{:S(2)}) collective-permute-start(f32[6,12,2,128]{3,2,1,0:T(2,128)S(1)} %get-tuple-element.187), channel_id=1, source_target_pairs={{4,0},{8,4},{12,8},{0,12},{5,1},{9,5},{13,9},{1,13},{6,2},{10,6},{... | collective-permute-start | bytes 221192 | tf_op jit(solution)/shard_map/ppermute | solution.py:15
  11.7 2.0 %collective-permute-done.2 = f32[6,12,2,128]{3,2,1,0:T(2,128)S(1)} collective-permute-done((f32[6,12,2,128]{3,2,1,0:T(2,128)S(1)}, f32[6,12,2,128]{3,2,1,0:T(2,128)S(1)}, u32[]{:S(2)}, u32[]{:S(2)}) %collective-permute-start.2) | collective-permute-done | bytes 73760 | tf_op jit(solution)/shard_map/ppermute | solution.py:14
  14.4 0.6 copy-done.6
  15.1 1.2 %fusion.77 = (f32[6,12,20,2]{3,2,1,0:T(8,128)}, f32[6,12,20,2]{3,2,1,0:T(8,128)S(1)}) fusion(f32[6,12,20,128]{3,2,1,0:T(8,128)S(1)} %pad_maximum_fusion.1), kind=kLoop, calls=%fused_computation.127 | loop fusion | bytes 46080 | tf_op jit(solution)/shard_map/slice | solution.py:12
  16.4 1.7 %copy.102 = f32[6,12,20,2]{2,3,1,0:T(2,128)S(1)} copy(f32[6,12,20,2]{3,2,1,0:T(8,128)} %get-tuple-element.184) | data formatting | bytes 23040
  18.1 1.9 %collective-permute-start.4 = (f32[6,12,20,2]{2,3,1,0:T(2,128)S(1)}, f32[6,12,20,2]{2,3,1,0:T(2,128)S(1)}, u32[]{:S(2)}, u32[]{:S(2)}) collective-permute-start(f32[6,12,20,2]{2,3,1,0:T(2,128)S(1)} %copy.102), channel_id=1, source_target_pairs={{0,1},{1,2},{2,3},{3,0},{4,5},{5,6},{6,7},{7,4},{8,9},{9,10},{10,1... | collective-permute-start | bytes 34568 | tf_op jit(solution)/shard_map/ppermute | solution.py:14
  20.6 2.1 %collective-permute-start.5 = (f32[6,12,20,2]{2,3,1,0:T(2,128)S(1)}, f32[6,12,20,2]{2,3,1,0:T(2,128)S(1)}, u32[]{:S(2)}, u32[]{:S(2)}) collective-permute-start(f32[6,12,20,2]{2,3,1,0:T(2,128)S(1)} %copy.103), channel_id=1, source_target_pairs={{1,0},{2,1},{3,2},{0,3},{5,4},{6,5},{7,6},{4,7},{9,8},{10,9},{11,1... | collective-permute-start | bytes 34568 | tf_op jit(solution)/shard_map/ppermute | solution.py:15
  22.7 2.2 %collective-permute-done.4 = f32[6,12,20,2]{2,3,1,0:T(2,128)S(1)} collective-permute-done((f32[6,12,20,2]{2,3,1,0:T(2,128)S(1)}, f32[6,12,20,2]{2,3,1,0:T(2,128)S(1)}, u32[]{:S(2)}, u32[]{:S(2)}) %collective-permute-start.4) | collective-permute-done | bytes 11552 | tf_op jit(solution)/shard_map/ppermute | solution.py:14
  25.5 1.3 %collective-permute-done.5 = f32[6,12,20,2]{2,3,1,0:T(2,128)S(1)} collective-permute-done((f32[6,12,20,2]{2,3,1,0:T(2,128)S(1)}, f32[6,12,20,2]{2,3,1,0:T(2,128)S(1)}, u32[]{:S(2)}, u32[]{:S(2)}) %collective-permute-start.5) | collective-permute-done | bytes 11552 | tf_op jit(solution)/shard_map/ppermute | solution.py:15
  26.7 1.5 %copy.72 = f32[6,12,20,2]{3,2,1,0:T(8,128)} copy(f32[6,12,20,2]{2,3,1,0:T(2,128)S(1)} %collective-permute-done.5) | data formatting | bytes 23040 | tf_op jit(solution)/shard_map/ppermute | solution.py:15
  28.2 1.6 %pad_maximum_fusion.2 = f32[6,8,16,132]{3,2,1,0:T(8,128)S(1)} fusion(f32[6,12,20,2]{3,2,1,0:T(8,128)} %copy.72, f32[6,12,20,2]{3,2,1,0:T(8,128)S(1)} %copy.71, f32[6,12,2,128]{3,2,1,0:T(2,128)} %copy-done.6, f32[6,12,2,128]{3,2,1,0:T(2,128)} %copy-done.5, f32[6,2,16,128]{3,2,1,0:T(8,128)S(1)} %collective-permute-done.1, ...), kind=kLoop, calls=%fused_computation.30 | loop fusion | flops 608256 | bytes 1165824 | tf_op jit(solution)/shard_map/concatenate | solution.py:16
  29.7 1.5 %broadcast_in_dim.13 = f32[32,16384]{1,0:T(8,128)} broadcast(f32[]{:T(128)} %constant.103.clone.1), dimensions={} | broadcast | bytes 2097156 | tf_op jit(solution)/shard_map/broadcast_in_dim | solution.py:82
  31.2 26.2 %while.16 = (s32[]{:T(128)}, f32[32,16384]{1,0:T(8,128)}, f32[32,32]{1,0:T(8,128)S(1)}, f32[6,12,16,128]{3,2,1,0:T(8,128)S(1)}, f32[6,8,20,128]{3,2,1,0:T(8,128)...) while((s32[]{:T(128)}, f32[32,16384]{1,0:T(8,128)}, ...), condition=%wide.region_1.0_spmd.clone, body=%wide.region_0.0_spmd.clone.sunk | while | flops 178583568 | bytes 18319992 | solution.py:84
  32.6 1.3 %mul.118 = f32[81,4096]{1,0:T(8,128)} reshape(f32[9,9,4096]{2,1,0:T(8,128)S(1)} %broadcast_multiply_fusion.2) | data formatting | bytes 2654208 | tf_op jit(solution)/shard_map/while/body/eval_jaxpr/mul | solution.py:43
  33.9 3.3 %bitcast_dynamic-update-slice_fusion.2 = (f32[32,16384]{1,0:T(8,128)}, f32[4096,32]{0,1:T(8,128)S(1)}) fusion(f32[32,16384]{1,0:T(8,128)} %get-tuple-element.263, s32[]{:T(128)S(6)} %select_n.69, f32[81,4096]{1,0:T(8,128)} %mul.118, f32[32,81]{1,0:T(8,128)S(1)} %get-tuple-element.285), kind=kOutput, calls=%fused_computation.2.clone.1 | convolution fusion | flops 127401984 | bytes 2500740 | tf_op jit(solution)/shard_map/while/body/eval_jaxpr/dot_general | solution.py:44
  39.1 1.3 %mul.118 = f32[81,4096]{1,0:T(8,128)} reshape(f32[9,9,4096]{2,1,0:T(8,128)S(1)} %broadcast_multiply_fusion.2) | data formatting | bytes 2654208 | tf_op jit(solution)/shard_map/while/body/eval_jaxpr/mul | solution.py:43
  40.4 3.3 %bitcast_dynamic-update-slice_fusion.2 = (f32[32,16384]{1,0:T(8,128)}, f32[4096,32]{0,1:T(8,128)S(1)}) fusion(f32[32,16384]{1,0:T(8,128)} %get-tuple-element.263, s32[]{:T(128)S(6)} %select_n.69, f32[81,4096]{1,0:T(8,128)} %mul.118, f32[32,81]{1,0:T(8,128)S(1)} %get-tuple-element.285), kind=kOutput, calls=%fused_computation.2.clone.1 | convolution fusion | flops 127401984 | bytes 2500740 | tf_op jit(solution)/shard_map/while/body/eval_jaxpr/dot_general | solution.py:44
  43.7 0.6 convolution_add_fusion.7
  45.7 1.3 %mul.118 = f32[81,4096]{1,0:T(8,128)} reshape(f32[9,9,4096]{2,1,0:T(8,128)S(1)} %broadcast_multiply_fusion.2) | data formatting | bytes 2654208 | tf_op jit(solution)/shard_map/while/body/eval_jaxpr/mul | solution.py:43
  47.0 3.3 %bitcast_dynamic-update-slice_fusion.2 = (f32[32,16384]{1,0:T(8,128)}, f32[4096,32]{0,1:T(8,128)S(1)}) fusion(f32[32,16384]{1,0:T(8,128)} %get-tuple-element.263, s32[]{:T(128)S(6)} %select_n.69, f32[81,4096]{1,0:T(8,128)} %mul.118, f32[32,81]{1,0:T(8,128)S(1)} %get-tuple-element.285), kind=kOutput, calls=%fused_computation.2.clone.1 | convolution fusion | flops 127401984 | bytes 2500740 | tf_op jit(solution)/shard_map/while/body/eval_jaxpr/dot_general | solution.py:44
  52.3 1.3 %mul.118 = f32[81,4096]{1,0:T(8,128)} reshape(f32[9,9,4096]{2,1,0:T(8,128)S(1)} %broadcast_multiply_fusion.2) | data formatting | bytes 2654208 | tf_op jit(solution)/shard_map/while/body/eval_jaxpr/mul | solution.py:43
  53.6 3.3 %bitcast_dynamic-update-slice_fusion.2 = (f32[32,16384]{1,0:T(8,128)}, f32[4096,32]{0,1:T(8,128)S(1)}) fusion(f32[32,16384]{1,0:T(8,128)} %get-tuple-element.263, s32[]{:T(128)S(6)} %select_n.69, f32[81,4096]{1,0:T(8,128)} %mul.118, f32[32,81]{1,0:T(8,128)S(1)} %get-tuple-element.285), kind=kOutput, calls=%fused_computation.2.clone.1 | convolution fusion | flops 127401984 | bytes 2500740 | tf_op jit(solution)/shard_map/while/body/eval_jaxpr/dot_general | solution.py:44
  57.5 2.9 %cholesky.119 = f32[32,32]{1,0:T(8,128)S(1)} custom-call(f32[32,32]{1,0:T(8,128)S(1)} %fusion.21), custom_call_target="Cholesky" | custom-call | tf_op jit(solution)/shard_map/jit(cholesky)/cholesky | solution.py:54
  60.5 0.7 compare_reduce_fusion.6
  61.2 0.7 fusion.36
  61.9 0.6 collective-permute-start.6
  62.5 0.8 fusion.37
  63.4 2.3 %collective-permute-done.6 = f32[32,32]{0,1:T(8,128)S(1)} collective-permute-done((f32[32,32]{0,1:T(8,128)S(1)}, f32[32,32]{0,1:T(8,128)S(1)}, u32[]{:S(2)}, u32[]{:S(2)}) %collective-permute-start.6) | collective-permute-done | bytes 4128 | tf_op jit(solution)/shard_map/ppermute | solution.py:23
  65.9 2.9 %cholesky.130 = f32[32,32]{1,0:T(8,128)S(1)} custom-call(f32[32,32]{1,0:T(8,128)S(1)} %fusion.20), custom_call_target="Cholesky" | custom-call | tf_op jit(solution)/shard_map/jit(cholesky)/cholesky | solution.py:54
  68.9 0.7 compare_reduce_fusion.5
  69.6 0.7 fusion.38
  70.3 1.4 %collective-permute-start.7 = (f32[32,32]{0,1:T(8,128)S(1)}, f32[32,32]{0,1:T(8,128)S(1)}, u32[]{:S(2)}, u32[]{:S(2)}) collective-permute-start(f32[32,32]{0,1:T(8,128)S(1)} %fusion.38), channel_id=1, source_target_pairs={{0,2},{1,3},{2,0},{3,1},{4,6},{5,7},{6,4},{7,5},{8,10},{9,11},{10,... | collective-permute-start | bytes 12296 | tf_op jit(solution)/shard_map/ppermute | solution.py:23
  71.7 0.8 fusion.39
  72.6 2.6 %collective-permute-done.7 = f32[32,32]{0,1:T(8,128)S(1)} collective-permute-done((f32[32,32]{0,1:T(8,128)S(1)}, f32[32,32]{0,1:T(8,128)S(1)}, u32[]{:S(2)}, u32[]{:S(2)}) %collective-permute-start.7) | collective-permute-done | bytes 4128 | tf_op jit(solution)/shard_map/ppermute | solution.py:23
  75.4 2.9 %cholesky.141 = f32[32,32]{1,0:T(8,128)S(1)} custom-call(f32[32,32]{1,0:T(8,128)S(1)} %fusion.19), custom_call_target="Cholesky" | custom-call | tf_op jit(solution)/shard_map/jit(cholesky)/cholesky | solution.py:54
  78.4 0.7 compare_reduce_fusion.4
  79.1 0.7 fusion.40
  79.9 0.8 fusion.41
  81.3 2.9 %cholesky.152 = f32[32,32]{1,0:T(8,128)S(1)} custom-call(f32[32,32]{1,0:T(8,128)S(1)} %fusion.18), custom_call_target="Cholesky" | custom-call | tf_op jit(solution)/shard_map/jit(cholesky)/cholesky | solution.py:54
  84.3 0.7 compare_reduce_fusion.3
  85.0 0.7 fusion.42
  85.7 0.7 collective-permute-start.9
  86.4 0.8 fusion.43
  87.2 2.2 %collective-permute-done.9 = f32[32,32]{0,1:T(8,128)S(1)} collective-permute-done((f32[32,32]{0,1:T(8,128)S(1)}, f32[32,32]{0,1:T(8,128)S(1)}, u32[]{:S(2)}, u32[]{:S(2)}) %collective-permute-start.9) | collective-permute-done | bytes 4128 | tf_op jit(solution)/shard_map/ppermute | solution.py:23
  89.7 2.9 %cholesky.163 = f32[32,32]{1,0:T(8,128)S(1)} custom-call(f32[32,32]{1,0:T(8,128)S(1)} %fusion.17), custom_call_target="Cholesky" | custom-call | tf_op jit(solution)/shard_map/jit(cholesky)/cholesky | solution.py:54
  92.7 0.7 compare_reduce_fusion.2
  93.4 0.7 fusion.44
  94.1 1.7 %collective-permute-start.10 = (f32[32,32]{0,1:T(8,128)S(1)}, f32[32,32]{0,1:T(8,128)S(1)}, u32[]{:S(2)}, u32[]{:S(2)}) collective-permute-start(f32[32,32]{0,1:T(8,128)S(1)} %fusion.44), channel_id=1, source_target_pairs={{0,16},{1,17},{2,18},{3,19},{4,20},{5,21},{6,22},{7,23},{8,24},{9,... | collective-permute-start | bytes 12296 | tf_op jit(solution)/shard_map/ppermute | solution.py:23
  95.8 0.8 fusion.45
  96.6 1.3 %collective-permute-done.10 = f32[32,32]{0,1:T(8,128)S(1)} collective-permute-done((f32[32,32]{0,1:T(8,128)S(1)}, f32[32,32]{0,1:T(8,128)S(1)}, u32[]{:S(2)}, u32[]{:S(2)}) %collective-permute-start.10) | collective-permute-done | bytes 4128 | tf_op jit(solution)/shard_map/ppermute | solution.py:23
  98.1 2.9 %cholesky.174 = f32[32,32]{1,0:T(8,128)S(1)} custom-call(f32[32,32]{1,0:T(8,128)S(1)} %fusion.16), custom_call_target="Cholesky" | custom-call | tf_op jit(solution)/shard_map/jit(cholesky)/cholesky | solution.py:54
  101.1 0.7 compare_reduce_fusion.1
  101.8 0.8 convolution_multiply_fusion
  102.7 2.9 %cholesky.185 = f32[32,32]{1,0:T(8,128)S(1)} custom-call(f32[32,32]{1,0:T(8,128)S(1)} %fusion.15), custom_call_target="Cholesky" | custom-call | tf_op jit(solution)/shard_map/jit(cholesky)/cholesky | solution.py:92
  105.7 0.7 compare_reduce_fusion
  106.4 0.7 fusion.12
  107.1 2.4 %custom-call.6 = f32[1,32,32]{1,2,0:T(8,128)S(1)} custom-call(f32[1,32,32]{2,1,0:T(8,128)S(1)} %fusion.12), custom_call_target="InvertDiagBlocksLowerTriangular" | custom-call | tf_op jit(solution)/shard_map/jit(_solve_triangular)/triangular_solve | solution.py:93
  109.8 3.5 %convolution_bitcast_fusion = f32[4,8,128,128]{3,1,2,0:T(8,128)S(1)} fusion(f32[32,32]{1,0:T(8,128)S(1)} %fusion.13, f32[32,16384]{1,0:T(8,128)} %get-tuple-element.132), kind=kOutput, calls=%fused_computation.22 | convolution fusion | flops 201326592 | bytes 4198400 | tf_op jit(solution)/shard_map/dot_general | solution.py:50
  113.2 1.7 %copy.104 = f32[4,8,128,128]{3,2,1,0:T(8,128)} copy(f32[4,8,128,128]{3,1,2,0:T(8,128)S(1)} %convolution_bitcast_fusion) | data formatting | bytes 4194304
  (116 shorter events, 11.2 us)
Async XLA Ops:
  1.9 6.5 %collective-permute-start = (f32[6,2,16,128]{3,2,1,0:T(8,128)S(1)}, f32[6,2,16,128]{3,2,1,0:T(8,128)S(1)}, u32[]{:S(2)}, u32[]{:S(2)}) collective-permute-start(f32[6,2,16,128]{3,2,1,0:T(8,128)S(1)} %get-tuple-element.188), channel_id=1, source_target_pairs={{0,16},{16,0},{1,17},{17,1},{2,18},{18,2},{3,19},{19,3},{4,20},{20... | collective-permute-start | bytes 294920 | tf_op jit(solution)/shard_map/ppermute | solution.py:14
  4.9 4.9 %collective-permute-start.1 = (f32[6,2,16,128]{3,2,1,0:T(8,128)S(1)}, f32[6,2,16,128]{3,2,1,0:T(8,128)S(1)}, u32[]{:S(2)}, u32[]{:S(2)}) collective-permute-start(f32[6,2,16,128]{3,2,1,0:T(8,128)S(1)} %get-tuple-element.189), channel_id=1, source_target_pairs={{16,0},{0,16},{17,1},{1,17},{18,2},{2,18},{19,3},{3,19},{20,4},{4,... | collective-permute-start | bytes 294920 | tf_op jit(solution)/shard_map/ppermute | solution.py:15
  9.9 3.8 %collective-permute-start.2 = (f32[6,12,2,128]{3,2,1,0:T(2,128)S(1)}, f32[6,12,2,128]{3,2,1,0:T(2,128)S(1)}, u32[]{:S(2)}, u32[]{:S(2)}) collective-permute-start(f32[6,12,2,128]{3,2,1,0:T(2,128)S(1)} %get-tuple-element.186), channel_id=1, source_target_pairs={{0,4},{4,8},{8,12},{12,0},{1,5},{5,9},{9,13},{13,1},{2,6},{6,10},{... | collective-permute-start | bytes 221192 | tf_op jit(solution)/shard_map/ppermute | solution.py:14
  10.0 3.9 %collective-permute-start.3 = (f32[6,12,2,128]{3,2,1,0:T(2,128)S(1)}, f32[6,12,2,128]{3,2,1,0:T(2,128)S(1)}, u32[]{:S(2)}, u32[]{:S(2)}) collective-permute-start(f32[6,12,2,128]{3,2,1,0:T(2,128)S(1)} %get-tuple-element.187), channel_id=1, source_target_pairs={{4,0},{8,4},{12,8},{0,12},{5,1},{9,5},{13,9},{1,13},{6,2},{10,6},{... | collective-permute-start | bytes 221192 | tf_op jit(solution)/shard_map/ppermute | solution.py:15
  13.8 0.6 copy-start.5
  14.4 0.6 copy-start.6
  18.1 6.9 %collective-permute-start.4 = (f32[6,12,20,2]{2,3,1,0:T(2,128)S(1)}, f32[6,12,20,2]{2,3,1,0:T(2,128)S(1)}, u32[]{:S(2)}, u32[]{:S(2)}) collective-permute-start(f32[6,12,20,2]{2,3,1,0:T(2,128)S(1)} %copy.102), channel_id=1, source_target_pairs={{0,1},{1,2},{2,3},{3,0},{4,5},{5,6},{6,7},{7,4},{8,9},{9,10},{10,1... | collective-permute-start | bytes 34568 | tf_op jit(solution)/shard_map/ppermute | solution.py:14
  20.6 6.2 %collective-permute-start.5 = (f32[6,12,20,2]{2,3,1,0:T(2,128)S(1)}, f32[6,12,20,2]{2,3,1,0:T(2,128)S(1)}, u32[]{:S(2)}, u32[]{:S(2)}) collective-permute-start(f32[6,12,20,2]{2,3,1,0:T(2,128)S(1)} %copy.103), channel_id=1, source_target_pairs={{1,0},{2,1},{3,2},{0,3},{5,4},{6,5},{7,6},{4,7},{9,8},{10,9},{11,1... | collective-permute-start | bytes 34568 | tf_op jit(solution)/shard_map/ppermute | solution.py:15
  28.2 3.0 %copy-start.4 = (f32[32,81]{1,0:T(8,128)S(1)}, f32[32,81]{1,0:T(8,128)}, u32[]{:S(2)}) copy-start(f32[32,81]{1,0:T(8,128)} %param.8) | copy-start | bytes 31108
  31.2 0.8 copy-start
  31.2 1.1 copy-start.2
  33.9 3.9 %copy-start.1 = (f32[6,8,20,128]{3,2,1,0:T(8,128)S(1)}, f32[6,8,20,128]{3,2,1,0:T(8,128)}, u32[]{:S(2)}) copy-start(f32[6,8,20,128]{3,2,1,0:T(8,128)} %copy-done) | copy-start | bytes 1474564 | tf_op jit(solution)/shard_map/while
  33.9 3.9 %copy-start.3 = (f32[6,8,16,132]{3,2,1,0:T(8,128)S(1)}, f32[6,8,16,132]{3,2,1,0:T(8,128)}, u32[]{:S(2)}) copy-start(f32[6,8,16,132]{3,2,1,0:T(8,128)} %copy-done.2) | copy-start | bytes 1216516 | tf_op jit(solution)/shard_map/while
  37.8 0.8 copy-start
  37.8 1.1 copy-start.2
  40.4 3.9 %copy-start.1 = (f32[6,8,20,128]{3,2,1,0:T(8,128)S(1)}, f32[6,8,20,128]{3,2,1,0:T(8,128)}, u32[]{:S(2)}) copy-start(f32[6,8,20,128]{3,2,1,0:T(8,128)} %copy-done) | copy-start | bytes 1474564 | tf_op jit(solution)/shard_map/while
  40.4 3.9 %copy-start.3 = (f32[6,8,16,132]{3,2,1,0:T(8,128)S(1)}, f32[6,8,16,132]{3,2,1,0:T(8,128)}, u32[]{:S(2)}) copy-start(f32[6,8,16,132]{3,2,1,0:T(8,128)} %copy-done.2) | copy-start | bytes 1216516 | tf_op jit(solution)/shard_map/while
  44.3 0.8 copy-start
  44.3 1.1 copy-start.2
  47.0 3.9 %copy-start.1 = (f32[6,8,20,128]{3,2,1,0:T(8,128)S(1)}, f32[6,8,20,128]{3,2,1,0:T(8,128)}, u32[]{:S(2)}) copy-start(f32[6,8,20,128]{3,2,1,0:T(8,128)} %copy-done) | copy-start | bytes 1474564 | tf_op jit(solution)/shard_map/while
  47.0 3.9 %copy-start.3 = (f32[6,8,16,132]{3,2,1,0:T(8,128)S(1)}, f32[6,8,16,132]{3,2,1,0:T(8,128)}, u32[]{:S(2)}) copy-start(f32[6,8,16,132]{3,2,1,0:T(8,128)} %copy-done.2) | copy-start | bytes 1216516 | tf_op jit(solution)/shard_map/while
  50.9 0.8 copy-start
  50.9 1.1 copy-start.2
  53.6 3.9 %copy-start.1 = (f32[6,8,20,128]{3,2,1,0:T(8,128)S(1)}, f32[6,8,20,128]{3,2,1,0:T(8,128)}, u32[]{:S(2)}) copy-start(f32[6,8,20,128]{3,2,1,0:T(8,128)} %copy-done) | copy-start | bytes 1474564 | tf_op jit(solution)/shard_map/while
  53.6 3.9 %copy-start.3 = (f32[6,8,16,132]{3,2,1,0:T(8,128)S(1)}, f32[6,8,16,132]{3,2,1,0:T(8,128)}, u32[]{:S(2)}) copy-start(f32[6,8,16,132]{3,2,1,0:T(8,128)} %copy-done.2) | copy-start | bytes 1216516 | tf_op jit(solution)/shard_map/while
  61.9 3.8 %collective-permute-start.6 = (f32[32,32]{0,1:T(8,128)S(1)}, f32[32,32]{0,1:T(8,128)S(1)}, u32[]{:S(2)}, u32[]{:S(2)}) collective-permute-start(f32[32,32]{0,1:T(8,128)S(1)} %fusion.36), channel_id=1, source_target_pairs={{0,1},{1,0},{2,3},{3,2},{4,5},{5,4},{6,7},{7,6},{8,9},{9,8},{10,11... | collective-permute-start | bytes 12296 | tf_op jit(solution)/shard_map/ppermute | solution.py:23
  70.3 4.9 %collective-permute-start.7 = (f32[32,32]{0,1:T(8,128)S(1)}, f32[32,32]{0,1:T(8,128)S(1)}, u32[]{:S(2)}, u32[]{:S(2)}) collective-permute-start(f32[32,32]{0,1:T(8,128)S(1)} %fusion.38), channel_id=1, source_target_pairs={{0,2},{1,3},{2,0},{3,1},{4,6},{5,7},{6,4},{7,5},{8,10},{9,11},{10,... | collective-permute-start | bytes 12296 | tf_op jit(solution)/shard_map/ppermute | solution.py:23
  79.8 1.2 %collective-permute-start.8 = (f32[32,32]{0,1:T(8,128)S(1)}, f32[32,32]{0,1:T(8,128)S(1)}, u32[]{:S(2)}, u32[]{:S(2)}) collective-permute-start(f32[32,32]{0,1:T(8,128)S(1)} %fusion.40), channel_id=1, source_target_pairs={{0,4},{1,5},{2,6},{3,7},{4,0},{5,1},{6,2},{7,3},{8,12},{9,13},{10,... | collective-permute-start | bytes 12296 | tf_op jit(solution)/shard_map/ppermute | solution.py:23
  85.7 3.8 %collective-permute-start.9 = (f32[32,32]{0,1:T(8,128)S(1)}, f32[32,32]{0,1:T(8,128)S(1)}, u32[]{:S(2)}, u32[]{:S(2)}) collective-permute-start(f32[32,32]{0,1:T(8,128)S(1)} %fusion.42), channel_id=1, source_target_pairs={{0,8},{1,9},{2,10},{3,11},{4,12},{5,13},{6,14},{7,15},{8,0},{9,1},... | collective-permute-start | bytes 12296 | tf_op jit(solution)/shard_map/ppermute | solution.py:23
  94.1 3.8 %collective-permute-start.10 = (f32[32,32]{0,1:T(8,128)S(1)}, f32[32,32]{0,1:T(8,128)S(1)}, u32[]{:S(2)}, u32[]{:S(2)}) collective-permute-start(f32[32,32]{0,1:T(8,128)S(1)} %fusion.44), channel_id=1, source_target_pairs={{0,16},{1,17},{2,18},{3,19},{4,20},{5,21},{6,22},{7,23},{8,24},{9,... | collective-permute-start | bytes 12296 | tf_op jit(solution)/shard_map/ppermute | solution.py:23
where the time goes:
time: 115 us
  other arithmetic  36 us (31%)
  matrix products  24.8 us (22%)
  local copies, waits for them, and re-layouts  20.7 us (18%)
  waiting for transfers between devices  19.3 us (17%)
  starting transfers between devices  13.4 us (12%)
    another operation x18, other arithmetic, upper_factor(): return jnp.linalg.cholesky(matrix).T  22.1 us
    dot_general x4, matrix products, snapshots(): jnp.dot(weights, products, precision=lax.Precision.HIGHEST, preferred_ele...  13.1 us
    dot_general x16, matrix products, inner(): jnp.dot(left, right, precision=lax.Precision.HIGHEST, preferred_element_t...  11.5 us
    ppermute x5, waiting for transfers between devices, partner_2(): return lax.ppermute(value, axis, pairs)  8.79 us
    ppermute x3, waiting for transfers between devices, padded_2(): before = lax.ppermute(last, axis, up)  7.69 us
    unnamed x10, local copies, waits for them, and re-layouts  5.97 us
    mul x12, local copies, waits for them, and re-layouts, snapshots(): products = (grads[:9][:, None, :] * grads[9:][None, :, :]).reshape(81, -1)  5.43 us
    ppermute x3, starting transfers between devices, padded_2(): before = lax.ppermute(last, axis, up)  5 us
  transfers between devices with their start and end apart: 11, of which 11 were waited for; matrix products, arithmetic and copies ran while one was open for 5% of the time, Pallas kernels for 0%

commit v1 on v0

v1 whole, which is shorter than its diff:
```python
import functools

import jax
import jax.numpy as jnp
from jax import lax
from jax.experimental import pallas as pl
from jax.experimental.pallas import tpu as pltpu
from jax.sharding import PartitionSpec as P

MESH = pl.DeviceIdType.MESH
F32 = jnp.float32
BF16 = jnp.bfloat16
AXES = ("stream", "span", "depth")
VMEM = pl.BlockSpec(memory_space=pltpu.VMEM)
LIMIT = 48 * 1024 * 1024


def halo_kernel(sizes, f_ref, a_ref, hx, hy, hz, ysend, zsend, send, recv):
    ids = [lax.axis_index(name) for name in AXES]
    peers = []
    for name, size, me in zip(AXES, sizes, ids):
        peers.append({name: lax.rem(me + 1, size)})
        peers.append({name: lax.rem(me + size - 1, size)})
    barrier = pltpu.get_barrier_semaphore()
    for peer in peers:
        pl.semaphore_signal(barrier, inc=1, device_id=peer, device_id_type=MESH)

    planes, rows = f_ref.shape[1], f_ref.shape[2]
    half = 3 * planes
    for k, ref in enumerate((f_ref, a_ref)):
        flat = ref.reshape(half * rows, 128)
        for j in range(2):
            ysend[0, j, k * half:(k + 1) * half, :] = flat[pl.ds(rows - 2 + j, half, stride=rows), :]
            ysend[1, j, k * half:(k + 1) * half, :] = flat[pl.ds(j, half, stride=rows), :]

    pl.semaphore_wait(barrier, len(peers))
    copies = []

    def push(src, dst, peer):
        n = len(copies)
        copy = pltpu.make_async_remote_copy(
            src_ref=src, dst_ref=dst, send_sem=send.at[n], recv_sem=recv.at[n],
            device_id=peer, device_id_type=MESH)
        copy.start()
        copies.append(copy)

    for k, ref in enumerate((f_ref, a_ref)):
        push(ref.at[:, planes - 2:planes], hx.at[0, 3 * k:3 * k + 3], peers[0])
        push(ref.at[:, 0:2], hx.at[1, 3 * k:3 * k + 3], peers[1])
    push(ysend.at[0], hy.at[0], peers[2])
    push(ysend.at[1], hy.at[1], peers[3])

    lane = lax.broadcasted_iota(jnp.int32, (rows, 128), 1)
    for k, ref in enumerate((f_ref, a_ref)):
        last = jnp.zeros((rows, 128), F32)
        first = jnp.zeros((rows, 128), F32)
        for c in range(3):
            for x in range(planes):
                i = c * planes + x
                own = ref[c, x]
                head = jnp.where(lane == 0, -own, 8.0 * pltpu.roll(own, 1, 1) - own)
                tail = jnp.where(lane == 126, own - 8.0 * pltpu.roll(own, 127, 1), own)
                head = pltpu.roll(head, 4 * i, 1) if i else head
                tail = pltpu.roll(tail, (4 * i + 4) % 128, 1)
                first = jnp.where(lane // 4 == i, head, first)
                last = jnp.where(lane // 4 == i, tail, last)
        zsend[0, k] = last
        zsend[1, k] = first
    push(zsend.at[0], hz.at[0], peers[4])
    push(zsend.at[1], hz.at[1], peers[5])
    for copy in copies:
        copy.wait()


def split(value):
    high = value.astype(BF16)
    low = (value - high.astype(F32)).astype(BF16)
    return high, low


def snap_kernel(f_ref, a_ref, hx, hy, hz, w_ref, s_ref, g_ref, px, py, gs, rhs, lhs, acc):
    planes, rows = f_ref.shape[1], f_ref.shape[2]
    half = 3 * planes
    cells = rows * 128
    row = lax.broadcasted_iota(jnp.int32, (81, 176), 0)
    col = lax.broadcasted_iota(jnp.int32, (81, 176), 1)
    block, r = col // 16, col % 8
    source = jnp.where(block < 9, block * 9 + r, jnp.where(block == 9, r * 9 + 8, 80))
    keep = (row == source) & ((block < 10) | (r == 0))
    pick = jnp.where(keep, 1.0, 0.0).astype(BF16)
    w_high, w_low = split(w_ref[...] * (1.0 / 144.0))
    lhs[0:32, :] = jnp.dot(w_high, pick, preferred_element_type=F32).astype(BF16)
    lhs[32:64, :] = jnp.dot(w_low, pick, preferred_element_type=F32).astype(BF16)

    for k, ref in enumerate((f_ref, a_ref)):
        px[3 * k:3 * k + 3, 2:planes + 2] = ref[...]
        for c in range(3):
            py[(3 * k + c) * planes:(3 * k + c + 1) * planes, 8:8 + rows, :] = ref[c]
    px[:, 0:2] = hx[0]
    px[:, planes + 2:planes + 4] = hx[1]
    flat = py.reshape(2 * half * (rows + 16), 128)
    for j in range(2):
        flat[pl.ds(6 + j, 2 * half, stride=rows + 16), :] = hy[0, j]
        flat[pl.ds(8 + rows + j, 2 * half, stride=rows + 16), :] = hy[1, j]

    lane = lax.broadcasted_iota(jnp.int32, (rows, 128), 1)
    acc[...] = jnp.zeros_like(acc)

    def stencil(m2, m1, p1, p2):
        return 8.0 * (p1 - m1) - (p2 - m2)

    @pl.loop(0, planes)
    def _(x):
        for k in range(2):
            halo_z = jnp.where(lane % 4 < 2, hz[1, k], hz[0, k])
            for c in range(3):
                m = 3 * k + c
                own = px[m, x + 2]
                dx = stencil(px[m, x], px[m, x + 1], px[m, x + 3], px[m, x + 4])
                i = m * planes + x
                dy = stencil(*[py[i, 8 + o:8 + o + rows, :] for o in (-2, -1, 1, 2)])
                p1 = jnp.where(lane == 127, 0.0, pltpu.roll(own, 127, 1))
                p2 = jnp.where(lane >= 126, 0.0, pltpu.roll(own, 126, 1))
                m1 = jnp.where(lane == 0, 0.0, pltpu.roll(own, 1, 1))
                m2 = jnp.where(lane <= 1, 0.0, pltpu.roll(own, 2, 1))
                edge = pltpu.roll(halo_z, lax.rem(254 - 4 * (c * planes + x), 128), 1)
                dz = stencil(m2, m1, p1, p2) + jnp.where((lane < 2) | (lane >= 126), edge, 0.0)
                for d, slope in enumerate((dx, dy, dz)):
                    gs[pl.ds(16 * k + 3 * c + d, rows, stride=32), :] = slope
        for y in range(rows):
            base = 32 * y
            f8 = gs[base:base + 8, :]
            a8 = gs[base + 16:base + 24, :]
            a_end = gs[base + 24:base + 25, :]
            for n in range(11):
                if n < 9:
                    part = gs[base + n:base + n + 1, :] * a8
                elif n == 9:
                    part = f8 * a_end
                else:
                    part = jnp.broadcast_to(gs[base + 8:base + 9, :] * a_end, (8, 128))
                high = part.astype(BF16).astype(F32)
                both = jnp.concatenate([high, part - high], axis=0).astype(BF16)
                rhs[16 * n:16 * n + 16, 128 * y:128 * y + 128] = both
        wide = jnp.dot(lhs[...], rhs[...], preferred_element_type=F32)
        high, low = split(wide[:32] + wide[32:])
        both = jnp.concatenate([high, low], axis=0)
        s_ref[:, pl.ds(pl.multiple_of(x * cells, cells), cells)] = both
        acc[...] += lax.dot_general(both, both, (((1,), (1,)), ((), ())), preferred_element_type=F32)

    total = acc[0:32, :] + acc[32:64, :]
    gram = total[:, :32] + total[:, 32:]
    g_ref[...] = jnp.concatenate([gram[8 * q:8 * q + 8, :] for q in range(4)], axis=1)


def reduce_kernel(sizes, g_ref, t_ref, one, two, send1, recv1, send2, recv2):
    n_s, n_y, n_z = sizes
    i_s, i_y, i_z = [lax.axis_index(name) for name in AXES]
    count = n_s * n_y
    me = i_s * n_y + i_y

    def plane_peer(k):
        other = lax.rem(me + k, count)
        return other, {"stream": other // n_y, "span": lax.rem(other, n_y)}

    def depth_peer(k):
        other = lax.rem(i_z + k, n_z)
        return other, {"depth": other}

    barrier = pltpu.get_barrier_semaphore()
    for k in range(1, count):
        pl.semaphore_signal(barrier, inc=1, device_id=plane_peer(k)[1], device_id_type=MESH)
    for k in range(1, n_z):
        pl.semaphore_signal(barrier, inc=1, device_id=depth_peer(k)[1], device_id_type=MESH)
    one[me] = g_ref[...]
    pl.semaphore_wait(barrier, count - 1 + n_z - 1)

    def exchange(buf, mine, number, peer_of, send, recv):
        copies = []
        for k in range(1, number):
            copy = pltpu.make_async_remote_copy(
                src_ref=buf.at[mine], dst_ref=buf.at[mine], send_sem=send.at[k], recv_sem=recv.at[k],
                device_id=peer_of(k)[1], device_id_type=MESH)
            copy.start()
            copies.append(copy)
        for copy in copies:
            copy.wait()
        total = buf[0]
        for k in range(1, number):
            total = total + buf[k]
        return total

    two[i_z] = exchange(one, me, count, plane_peer, send1, recv1)
    t_ref[...] = exchange(two, i_z, n_z, depth_peer, send2, recv2)


def factor(gram):
    lane = lax.broadcasted_iota(jnp.int32, (32, 128), 1)
    row = lax.broadcasted_iota(jnp.int32, (32, 128), 0)
    work = jnp.where(lane < 32, gram, jnp.where(lane - 32 == row, 1.0, 0.0))
    scale = jnp.zeros((32, 128), F32)
    for base in range(0, 32, 8):
        cols = [jnp.broadcast_to(work[:, base + q:base + q + 1], (32, 128)) for q in range(8)]
        for q in range(8):
            j = base + q
            pivot = jnp.broadcast_to(cols[q][j:j + 1, :], (32, 128))
            ratio = jnp.where(row > j, cols[q] * (1.0 / pivot), 0.0)
            for t in range(q + 1, 8):
                cols[t] = cols[t] - ratio * cols[t][j:j + 1, :]
            work = work - ratio * work[j:j + 1, :]
            scale = jnp.where(row == j, pivot, scale)
    return pltpu.roll(work, 96, 1) * lax.rsqrt(scale)


def basis_kernel(cells, planes, t_ref, s_ref, o_ref, stage, sems):
    packed = t_ref[...] * (1.0 / cells)
    gram = jnp.concatenate([packed if q == 0 else pltpu.roll(packed, 128 - 32 * q, 1) for q in range(4)], axis=0)
    inverse = factor(gram)[:, :32]
    high, low = split(inverse)
    left = jnp.concatenate(
        [jnp.concatenate([high, high], axis=1), jnp.concatenate([low, low], axis=1)], axis=0)
    rows = o_ref.shape[2]
    flat = stage.reshape(32 * planes * rows, 128)
    copies = []
    for x in range(planes):
        wide = jnp.dot(left, s_ref[:, x * rows * 128:(x + 1) * rows * 128], preferred_element_type=F32)
        block = wide[:32] + wide[32:]
        for y in range(rows):
            flat[pl.ds(x * rows + y, 32, stride=planes * rows), :] = block[:, 128 * y:128 * y + 128]
        copy = pltpu.make_async_copy(stage.at[:, pl.ds(x * rows, rows), :], o_ref.at[:, x], sems.at[x])
        copy.start()
        copies.append(copy)
    for copy in copies:
        copy.wait()


def body(sizes, forward, adjoint, weights):
    _, planes, rows, depth = forward.shape
    half = 3 * planes
    plane_count = sizes[0] * sizes[1]
    cells = planes * rows * depth * plane_count * sizes[2]
    hx, hy, hz = pl.pallas_call(
        functools.partial(halo_kernel, sizes),
        out_shape=(
            jax.ShapeDtypeStruct((2, 6, 2, rows, depth), F32),
            jax.ShapeDtypeStruct((2, 2, 2 * half, depth), F32),
            jax.ShapeDtypeStruct((2, 2, rows, depth), F32)),
        in_specs=[VMEM] * 2,
        out_specs=(VMEM,) * 3,
        scratch_shapes=[
            pltpu.VMEM((2, 2, 2 * half, depth), F32),
            pltpu.VMEM((2, 2, rows, depth), F32),
            pltpu.SemaphoreType.DMA((8,)),
            pltpu.SemaphoreType.DMA((8,))],
        compiler_params=pltpu.CompilerParams(collective_id=0, has_side_effects=True, vmem_limit_bytes=LIMIT),
        name="halo",
    )(forward, adjoint)
    snaps, gram = pl.pallas_call(
        snap_kernel,
        out_shape=(
            jax.ShapeDtypeStruct((64, planes * rows * depth), BF16),
            jax.ShapeDtypeStruct((8, 128), F32)),
        in_specs=[VMEM] * 6,
        out_specs=(VMEM,) * 2,
        scratch_shapes=[
            pltpu.VMEM((6, planes + 4, rows, depth), F32),
            pltpu.VMEM((2 * half, rows + 16, depth), F32),
            pltpu.VMEM((rows * 32, depth), F32),
            pltpu.VMEM((176, rows * depth), BF16),
            pltpu.VMEM((64, 176), BF16),
            pltpu.VMEM((64, 64), F32)],
        compiler_params=pltpu.CompilerParams(vmem_limit_bytes=LIMIT),
        name="snap",
    )(forward, adjoint, hx, hy, hz, weights)
    total = pl.pallas_call(
        functools.partial(reduce_kernel, sizes),
        out_shape=jax.ShapeDtypeStruct((8, 128), F32),
        in_specs=[VMEM],
        out_specs=VMEM,
        scratch_shapes=[
            pltpu.VMEM((plane_count, 8, 128), F32),
            pltpu.VMEM((sizes[2], 8, 128), F32),
            pltpu.SemaphoreType.DMA((plane_count,)),
            pltpu.SemaphoreType.DMA((plane_count,)),
            pltpu.SemaphoreType.DMA((sizes[2],)),
            pltpu.SemaphoreType.DMA((sizes[2],))],
        compiler_params=pltpu.CompilerParams(collective_id=1, has_side_effects=True, vmem_limit_bytes=LIMIT),
        name="reduce",
    )(gram)
    return pl.pallas_call(
        functools.partial(basis_kernel, cells, planes),
        out_shape=jax.ShapeDtypeStruct((32, planes, rows, depth), F32),
        in_specs=[VMEM] * 2,
        out_specs=pl.BlockSpec(memory_space=pl.ANY),
        scratch_shapes=[
            pltpu.VMEM((32, planes * rows, depth), F32),
            pltpu.SemaphoreType.DMA((planes,))],
        compiler_params=pltpu.CompilerParams(vmem_limit_bytes=LIMIT),
        name="basis",
    )(total, snaps)


def solution(mesh):
    sizes = tuple(mesh.shape[name] for name in AXES)
    in_specs = (P(None, *AXES), P(None, *AXES), P())
    return jax.shard_map(
        functools.partial(body, sizes), mesh=mesh, in_specs=in_specs, out_specs=P(None, *AXES), check_vma=False)
```

time: 115 us -> 32.2 us (0.28)
  other arithmetic: 36 us -> 0 us
  Pallas kernels: 0 us -> 29.4 us
  matrix products: 24.8 us -> 0 us
  waiting for transfers between devices: 19.3 us -> 0 us
  local copies, waits for them, and re-layouts: 20.7 us -> 2.57 us
  starting transfers between devices: 13.4 us -> 0 us
    another operation x35 -> x0, other arithmetic: 29.8 us -> none  [the longest x18 22.1 us: upper_factor(): return jnp.linalg.cholesky(matrix).T]
    pallas_call x0 -> x4, Pallas kernels: none -> 29.4 us  [the longest x1 11.3 us: body(): pl.pallas_call(functools.partial(halo_kernel, sizes), out_shape=(jax.Shap...]
    dot_general x20 -> x0, matrix products: 24.5 us -> none  [the longest x4 13.1 us: snapshots(): jnp.dot(weights, products, precision=lax.Precision.HIGHEST, preferred_ele...]
    ppermute x11 -> x0, waiting for transfers between devices: 19.3 us -> none  [the longest x5 8.79 us: partner_2(): return lax.ppermute(value, axis, pairs)]
    ppermute x11 -> x0, starting transfers between devices: 13.4 us -> none  [the longest x3 5 us: padded_2(): before = lax.ppermute(last, axis, up)]
    mul x12 -> x0, local copies, waits for them, and re-layouts: 5.43 us -> none  [snapshots(): products = (grads[:9][:, None, :] * grads[9:][None, :, :]).reshape(81, -1)]
    transpose x5 -> x0, other arithmetic: 3.47 us -> none  [upper_factor(): return jnp.linalg.cholesky(matrix).T]
    unnamed x10 -> x6, local copies, waits for them, and re-layouts: 5.97 us -> 2.57 us
  transfers between devices with their start and end apart: 11 -> 0, of which waited for: 11 -> 0; matrix products, arithmetic and copies ran while one was open for 5% -> 0% of each run, Pallas kernels for 0% -> 0%
where the time goes in v1:
time: 32.2 us; the launch traced here: 32 us
  Pallas kernels  29.4 us (91%)
  local copies, waits for them, and re-layouts  2.57 us (8%)
    pallas_call x1, Pallas kernels, body(): pl.pallas_call(functools.partial(halo_kernel, sizes), out_shape=(jax.Shap...  11.3 us
    pallas_call x1, Pallas kernels, body(): pl.pallas_call(functools.partial(reduce_kernel, sizes), out_shape=jax.Sha...  8.9 us
    pallas_call x1, Pallas kernels, body(): pl.pallas_call(snap_kernel, out_shape=(jax.ShapeDtypeStruct((64, planes *...  5.86 us
    pallas_call x1, Pallas kernels, body(): pl.pallas_call(functools.partial(basis_kernel, cells, planes), out_shape=...  3.29 us
    unnamed x6, local copies, waits for them, and re-layouts  2.57 us

profile of v1, /device:TPU:0, one launch (start us, length us, event | category | flops | bytes accessed | tf_op | source)
XLA Modules:
  0.0 32.0 jit_solution(13748088323235826361)
XLA Ops:
  0.0 0.0 copy-start
  0.0 0.9 %copy-done = f32[3,8,16,128]{3,2,1,0:T(8,128)S(1)} copy-done((f32[3,8,16,128]{3,2,1,0:T(8,128)S(1)}, f32[3,8,16,128]{3,2,1,0:T(8,128)}, u32[]{:S(2)}) %copy-start) | copy-done | bytes 196632
  0.9 0.0 copy-start.1
  0.9 0.9 %copy-done.1 = f32[3,8,16,128]{3,2,1,0:T(8,128)S(1)} copy-done((f32[3,8,16,128]{3,2,1,0:T(8,128)S(1)}, f32[3,8,16,128]{3,2,1,0:T(8,128)}, u32[]{:S(2)}) %copy-start.1) | copy-done | bytes 196632
  1.9 11.3 %halo.1 = (f32[2,6,2,16,128]{4,3,2,1,0:T(8,128)S(1)}, f32[2,2,48,128]{3,2,1,0:T(8,128)S(1)}, f32[2,2,16,128]{3,2,1,0:T(8,128)S(1)}) custom-call(f32[3,8,16,128]{3,2,1,0:T(8,128)S(1)} %copy-done, f32[3,8,16,128]{3,2,1,0:T(8,128)S(1)} %copy-done.1), custom_call_target="tpu_custom_call" | custom-call | tf_op jit(solution)/shard_map/halo/pallas_call | solution.py:242
  13.2 0.0 copy-start.2
  13.2 0.7 %copy-done.2 = f32[32,81]{1,0:T(8,128)S(1)} copy-done((f32[32,81]{1,0:T(8,128)S(1)}, f32[32,81]{1,0:T(8,128)}, u32[]{:S(2)}) %copy-start.2) | copy-done | bytes 10392
  13.9 5.9 %snap.1 = (bf16[64,16384]{1,0:T(8,128)(2,1)S(1)}, f32[8,128]{1,0:T(8,128)S(1)}) custom-call(f32[3,8,16,128]{3,2,1,0:T(8,128)S(1)} %copy-done, f32[3,8,16,128]{3,2,1,0:T(8,128)S(1)} %copy-done.1, f32[2,6,2,16,128]{4,3,2,1,0:T(8,128)S(1)} %get-tuple-element.10.hx, f32[2,2,48,128]{3,2,1,0:T(8,128)S(1)} %get-tuple-element.11.hy, ...), custom_call_target="tpu_custom_call" | custom-call | tf_op jit(solution)/shard_map/snap/pallas_call | solution.py:258
  19.8 8.9 %reduce.1.t_ref = f32[8,128]{1,0:T(8,128)S(1)} custom-call(f32[8,128]{1,0:T(8,128)S(1)} %get-tuple-element.13.g_ref), custom_call_target="tpu_custom_call" | custom-call | tf_op jit(solution)/shard_map/reduce/pallas_call | solution.py:275
  28.7 3.3 %basis.1 = f32[32,8,16,128]{3,2,1,0:T(8,128)} custom-call(f32[8,128]{1,0:T(8,128)S(1)} %reduce.1.t_ref, bf16[64,16384]{1,0:T(8,128)(2,1)S(1)} %get-tuple-element.14.s_ref), custom_call_target="tpu_custom_call" | custom-call | tf_op jit(solution)/shard_map/basis/pallas_call | solution.py:290
Async XLA Ops:
  0.0 0.9 %copy-start = (f32[3,8,16,128]{3,2,1,0:T(8,128)S(1)}, f32[3,8,16,128]{3,2,1,0:T(8,128)}, u32[]{:S(2)}) copy-start(f32[3,8,16,128]{3,2,1,0:T(8,128)} %f_ref.3) | copy-start | bytes 589828
  0.9 0.9 %copy-start.1 = (f32[3,8,16,128]{3,2,1,0:T(8,128)S(1)}, f32[3,8,16,128]{3,2,1,0:T(8,128)}, u32[]{:S(2)}) copy-start(f32[3,8,16,128]{3,2,1,0:T(8,128)} %a_ref.3) | copy-start | bytes 589828
  13.2 0.7 %copy-start.2 = (f32[32,81]{1,0:T(8,128)S(1)}, f32[32,81]{1,0:T(8,128)}, u32[]{:S(2)}) copy-start(f32[32,81]{1,0:T(8,128)} %w_ref.1) | copy-start | bytes 31108

commit v2 on v1

v2 whole, which is shorter than its diff:
```python
import functools

import jax
import jax.numpy as jnp
from jax import lax
from jax.experimental import pallas as pl
from jax.experimental.pallas import tpu as pltpu
from jax.sharding import PartitionSpec as P

MESH = pl.DeviceIdType.MESH
F32 = jnp.float32
BF16 = jnp.bfloat16
AXES = ("stream", "span", "depth")
VMEM = pl.BlockSpec(memory_space=pltpu.VMEM)
LIMIT = 48 * 1024 * 1024


def split(value):
    high = value.astype(BF16)
    low = (value - high.astype(F32)).astype(BF16)
    return high, low


def snap_kernel(sizes, f_ref, a_ref, w_ref, s_ref, t_ref, px, py, hy, hz, ysend, zsend, wv, gs, rhs, lhs, acc,
                one, two, local, send, recv, send1, recv1, send2, recv2):
    n_s, n_y, n_z = sizes
    i_s, i_y, i_z = [lax.axis_index(name) for name in AXES]
    count = n_s * n_y
    me = i_s * n_y + i_y
    planes, rows = f_ref.shape[1], f_ref.shape[2]
    half = 3 * planes
    cells = rows * 128
    tall = rows + 16

    def plane_peer(k):
        other = lax.rem(me + k, count)
        return {"stream": other // n_y, "span": lax.rem(other, n_y)}

    def depth_peer(k):
        return {"depth": lax.rem(i_z + k, n_z)}

    barrier = pltpu.get_barrier_semaphore()
    for k in range(1, count):
        pl.semaphore_signal(barrier, inc=1, device_id=plane_peer(k), device_id_type=MESH)
    for k in range(1, n_z):
        pl.semaphore_signal(barrier, inc=1, device_id=depth_peer(k), device_id_type=MESH)

    loads = []

    def load(src, dst):
        copy = pltpu.make_async_copy(src, dst, local.at[len(loads)])
        copy.start()
        loads.append(copy)

    for k, ref in enumerate((f_ref, a_ref)):
        for c in range(3):
            m = 3 * k + c
            load(ref.at[c], py.at[m * planes:(m + 1) * planes, 8:8 + rows])
        load(ref, px.at[3 * k:3 * k + 3, 2:planes + 2])
    load(w_ref, wv)
    for copy in loads:
        copy.wait()

    flat = py.reshape(2 * half * tall, 128)
    for j in range(2):
        ysend[0, j] = flat[pl.ds(6 + rows + j, 2 * half, stride=tall), :]
        ysend[1, j] = flat[pl.ds(8 + j, 2 * half, stride=tall), :]
    lane = lax.broadcasted_iota(jnp.int32, (rows, 128), 1)
    for k in range(2):
        last = jnp.zeros((rows, 128), F32)
        first = jnp.zeros((rows, 128), F32)
        for i in range(half):
            own = py[k * half + i, 8:8 + rows, :]
            head = jnp.where(lane == 0, -own, 8.0 * pltpu.roll(own, 1, 1) - own)
            tail = jnp.where(lane == 126, own - 8.0 * pltpu.roll(own, 127, 1), own)
            head = pltpu.roll(head, 4 * i, 1) if i else head
            tail = pltpu.roll(tail, (4 * i + 4) % 128, 1)
            first = jnp.where(lane // 4 == i, head, first)
            last = jnp.where(lane // 4 == i, tail, last)
        zsend[0, k] = last
        zsend[1, k] = first

    pl.semaphore_wait(barrier, count - 1 + n_z - 1)
    copies = []

    def push(src, dst, peer):
        n = len(copies)
        copy = pltpu.make_async_remote_copy(
            src_ref=src, dst_ref=dst, send_sem=send.at[n], recv_sem=recv.at[n],
            device_id=peer, device_id_type=MESH)
        copy.start()
        copies.append(copy)

    def sides(name, size, mine):
        return {name: lax.rem(mine + 1, size)}, {name: lax.rem(mine + size - 1, size)}

    after_x, before_x = sides("stream", n_s, i_s)
    after_y, before_y = sides("span", n_y, i_y)
    after_z, before_z = sides("depth", n_z, i_z)
    push(ysend.at[0], hy.at[0], after_y)
    push(ysend.at[1], hy.at[1], before_y)
    push(zsend.at[0], hz.at[0], after_z)
    push(zsend.at[1], hz.at[1], before_z)
    for k, ref in enumerate((f_ref, a_ref)):
        push(ref.at[:, planes - 2:planes], px.at[3 * k:3 * k + 3, 0:2], after_x)
    for k, ref in enumerate((f_ref, a_ref)):
        push(ref.at[:, 0:2], px.at[3 * k:3 * k + 3, planes + 2:planes + 4], before_x)

    row = lax.broadcasted_iota(jnp.int32, (81, 176), 0)
    col = lax.broadcasted_iota(jnp.int32, (81, 176), 1)
    block, r = col // 16, col % 8
    source = jnp.where(block < 9, block * 9 + r, jnp.where(block == 9, r * 9 + 8, 80))
    keep = (row == source) & ((block < 10) | (r == 0))
    pick = jnp.where(keep, 1.0, 0.0).astype(BF16)
    w_high, w_low = split(wv[...] * (1.0 / 144.0))
    lhs[0:32, :] = jnp.dot(w_high, pick, preferred_element_type=F32).astype(BF16)
    lhs[32:64, :] = jnp.dot(w_low, pick, preferred_element_type=F32).astype(BF16)
    acc[...] = jnp.zeros_like(acc)

    for copy in copies[:4]:
        copy.wait()
    for j in range(2):
        flat[pl.ds(6 + j, 2 * half, stride=tall), :] = hy[0, j]
        flat[pl.ds(8 + rows + j, 2 * half, stride=tall), :] = hy[1, j]

    def stencil(m2, m1, p1, p2):
        return 8.0 * (p1 - m1) - (p2 - m2)

    def plane(x):
        for k in range(2):
            halo_z = jnp.where(lane % 4 < 2, hz[1, k], hz[0, k])
            for c in range(3):
                m = 3 * k + c
                own = px[m, x + 2]
                dx = stencil(px[m, x], px[m, x + 1], px[m, x + 3], px[m, x + 4])
                i = m * planes + x
                dy = stencil(*[py[i, 8 + o:8 + o + rows, :] for o in (-2, -1, 1, 2)])
                p1 = jnp.where(lane == 127, 0.0, pltpu.roll(own, 127, 1))
                p2 = jnp.where(lane >= 126, 0.0, pltpu.roll(own, 126, 1))
                m1 = jnp.where(lane == 0, 0.0, pltpu.roll(own, 1, 1))
                m2 = jnp.where(lane <= 1, 0.0, pltpu.roll(own, 2, 1))
                edge = pltpu.roll(halo_z, lax.rem(254 - 4 * (c * planes + x), 128), 1)
                dz = stencil(m2, m1, p1, p2) + jnp.where((lane < 2) | (lane >= 126), edge, 0.0)
                for d, slope in enumerate((dx, dy, dz)):
                    gs[pl.ds(16 * k + 3 * c + d, rows, stride=32), :] = slope
        for y in range(rows):
            base = 32 * y
            f8 = gs[base:base + 8, :]
            a8 = gs[base + 16:base + 24, :]
            a_end = gs[base + 24:base + 25, :]
            for n in range(11):
                if n < 9:
                    part = gs[base + n:base + n + 1, :] * a8
                elif n == 9:
                    part = f8 * a_end
                else:
                    part = jnp.broadcast_to(gs[base + 8:base + 9, :] * a_end, (8, 128))
                high = part.astype(BF16).astype(F32)
                both = jnp.concatenate([high, part - high], axis=0).astype(BF16)
                rhs[16 * n:16 * n + 16, 128 * y:128 * y + 128] = both
        wide = jnp.dot(lhs[...], rhs[...], preferred_element_type=F32)
        high, low = split(wide[:32] + wide[32:])
        both = jnp.concatenate([high, low], axis=0)
        s_ref[:, pl.ds(pl.multiple_of(x * cells, cells), cells)] = both
        acc[...] += lax.dot_general(both, both, (((1,), (1,)), ((), ())), preferred_element_type=F32)

    pl.loop(2, planes - 2)(plane)
    for copy in copies[4:6]:
        copy.wait()
    pl.loop(0, 2)(plane)
    for copy in copies[6:8]:
        copy.wait()
    pl.loop(planes - 2, planes)(plane)

    total = acc[0:32, :] + acc[32:64, :]
    gram = total[:, :32] + total[:, 32:]
    one[me] = jnp.concatenate([gram[8 * q:8 * q + 8, :] for q in range(4)], axis=1)

    def exchange(buf, mine, number, peer_of, send, recv):
        moves = []
        for k in range(1, number):
            copy = pltpu.make_async_remote_copy(
                src_ref=buf.at[mine], dst_ref=buf.at[mine], send_sem=send.at[k], recv_sem=recv.at[k],
                device_id=peer_of(k), device_id_type=MESH)
            copy.start()
            moves.append(copy)
        for copy in moves:
            copy.wait()
        total = buf[0]
        for k in range(1, number):
            total = total + buf[k]
        return total

    two[i_z] = exchange(one, me, count, plane_peer, send1, recv1)
    t_ref[...] = exchange(two, i_z, n_z, depth_peer, send2, recv2)


def factor(gram):
    lane = lax.broadcasted_iota(jnp.int32, (32, 128), 1)
    row = lax.broadcasted_iota(jnp.int32, (32, 128), 0)
    work = jnp.where(lane < 32, gram, jnp.where(lane - 32 == row, 1.0, 0.0))
    scale = jnp.zeros((32, 128), F32)
    for base in range(0, 32, 8):
        cols = [jnp.broadcast_to(work[:, base + q:base + q + 1], (32, 128)) for q in range(8)]
        for q in range(8):
            j = base + q
            pivot = jnp.broadcast_to(cols[q][j:j + 1, :], (32, 128))
            ratio = jnp.where(row > j, cols[q] * (1.0 / pivot), 0.0)
            for t in range(q + 1, 8):
                cols[t] = cols[t] - ratio * cols[t][j:j + 1, :]
            work = work - ratio * work[j:j + 1, :]
            scale = jnp.where(row == j, pivot, scale)
    return pltpu.roll(work, 96, 1) * lax.rsqrt(scale)


def basis_kernel(cells, planes, t_ref, s_ref, o_ref, stage, sems):
    packed = t_ref[...] * (1.0 / cells)
    gram = jnp.concatenate([packed if q == 0 else pltpu.roll(packed, 128 - 32 * q, 1) for q in range(4)], axis=0)
    inverse = factor(gram)[:, :32]
    high, low = split(inverse)
    left = jnp.concatenate(
        [jnp.concatenate([high, high], axis=1), jnp.concatenate([low, low], axis=1)], axis=0)
    rows = o_ref.shape[2]
    flat = stage.reshape(32 * planes * rows, 128)
    copies = []
    for x in range(planes):
        wide = jnp.dot(left, s_ref[:, x * rows * 128:(x + 1) * rows * 128], preferred_element_type=F32)
        block = wide[:32] + wide[32:]
        for y in range(rows):
            flat[pl.ds(x * rows + y, 32, stride=planes * rows), :] = block[:, 128 * y:128 * y + 128]
        copy = pltpu.make_async_copy(stage.at[:, pl.ds(x * rows, rows), :], o_ref.at[:, x], sems.at[x])
        copy.start()
        copies.append(copy)
    for copy in copies:
        copy.wait()


def body(sizes, forward, adjoint, weights):
    _, planes, rows, depth = forward.shape
    half = 3 * planes
    plane_count = sizes[0] * sizes[1]
    cells = planes * rows * depth * plane_count * sizes[2]
    total, snaps = pl.pallas_call(
        functools.partial(snap_kernel, sizes),
        out_shape=(
            jax.ShapeDtypeStruct((64, planes * rows * depth), BF16),
            jax.ShapeDtypeStruct((8, 128), F32)),
        in_specs=[pl.BlockSpec(memory_space=pltpu.HBM)] * 3,
        out_specs=(VMEM,) * 2,
        scratch_shapes=[
            pltpu.VMEM((6, planes + 4, rows, depth), F32),
            pltpu.VMEM((2 * half, rows + 16, depth), F32),
            pltpu.VMEM((2, 2, 2 * half, depth), F32),
            pltpu.VMEM((2, 2, rows, depth), F32),
            pltpu.VMEM((2, 2, 2 * half, depth), F32),
            pltpu.VMEM((2, 2, rows, depth), F32),
            pltpu.VMEM((32, 81), F32),
            pltpu.VMEM((rows * 32, depth), F32),
            pltpu.VMEM((176, rows * depth), BF16),
            pltpu.VMEM((64, 176), BF16),
            pltpu.VMEM((64, 64), F32),
            pltpu.VMEM((plane_count, 8, 128), F32),
            pltpu.VMEM((sizes[2], 8, 128), F32),
            pltpu.SemaphoreType.DMA((9,)),
            pltpu.SemaphoreType.DMA((8,)),
            pltpu.SemaphoreType.DMA((8,)),
            pltpu.SemaphoreType.DMA((plane_count,)),
            pltpu.SemaphoreType.DMA((plane_count,)),
            pltpu.SemaphoreType.DMA((sizes[2],)),
            pltpu.SemaphoreType.DMA((sizes[2],))],
        compiler_params=pltpu.CompilerParams(collective_id=0, has_side_effects=True, vmem_limit_bytes=LIMIT),
        name="snap",
    )(forward, adjoint, weights)[::-1]
    return pl.pallas_call(
        functools.partial(basis_kernel, cells, planes),
        out_shape=jax.ShapeDtypeStruct((32, planes, rows, depth), F32),
        in_specs=[VMEM] * 2,
        out_specs=pl.BlockSpec(memory_space=pl.ANY),
        scratch_shapes=[
            pltpu.VMEM((32, planes * rows, depth), F32),
            pltpu.SemaphoreType.DMA((planes,))],
        compiler_params=pltpu.CompilerParams(vmem_limit_bytes=LIMIT),
        name="basis",
    )(total, snaps)


def solution(mesh):
    sizes = tuple(mesh.shape[name] for name in AXES)
    in_specs = (P(None, *AXES), P(None, *AXES), P())
    return jax.shard_map(
        functools.partial(body, sizes), mesh=mesh, in_specs=in_specs, out_specs=P(None, *AXES), check_vma=False)
```

time: 32.2 us -> 28.8 us (0.89)
  Pallas kernels: 29.4 us -> 26 us
    pallas_call x3 -> x1, Pallas kernels: 26.1 us -> 22.7 us  [body(): pl.pallas_call(functools.partial(snap_kernel, sizes), out_shape=(jax.Shap...]
where the time goes in v2:
time: 28.8 us; the launch traced here: 28.5 us
  Pallas kernels  26 us (90%)
  local copies, waits for them, and re-layouts  2.57 us (9%)
    pallas_call x1, Pallas kernels, body(): pl.pallas_call(functools.partial(snap_kernel, sizes), out_shape=(jax.Shap...  22.7 us
    pallas_call x1, Pallas kernels, body(): pl.pallas_call(functools.partial(basis_kernel, cells, planes), out_shape=...  3.29 us
    unnamed x6, local copies, waits for them, and re-layouts  2.57 us

profile of v2, /device:TPU:0, one launch (start us, length us, event | category | flops | bytes accessed | tf_op | source)
XLA Modules:
  0.0 28.5 jit_solution(1666127033137411447)
XLA Ops:
  0.0 0.0 copy-start
  0.0 0.9 %copy-done = f32[3,8,16,128]{3,2,1,0:T(8,128)S(1)} copy-done((f32[3,8,16,128]{3,2,1,0:T(8,128)S(1)}, f32[3,8,16,128]{3,2,1,0:T(8,128)}, u32[]{:S(2)}) %copy-start) | copy-done | bytes 196632
  0.9 0.0 copy-start.1
  0.9 0.9 %copy-done.1 = f32[3,8,16,128]{3,2,1,0:T(8,128)S(1)} copy-done((f32[3,8,16,128]{3,2,1,0:T(8,128)S(1)}, f32[3,8,16,128]{3,2,1,0:T(8,128)}, u32[]{:S(2)}) %copy-start.1) | copy-done | bytes 196632
  1.9 0.0 copy-start.2
  1.9 0.7 %copy-done.2 = f32[32,81]{1,0:T(8,128)S(1)} copy-done((f32[32,81]{1,0:T(8,128)S(1)}, f32[32,81]{1,0:T(8,128)}, u32[]{:S(2)}) %copy-start.2) | copy-done | bytes 10392
  2.6 22.7 %snap.1 = (bf16[64,16384]{1,0:T(8,128)(2,1)S(1)}, f32[8,128]{1,0:T(8,128)S(1)}) custom-call(f32[3,8,16,128]{3,2,1,0:T(8,128)S(1)} %copy-done, f32[3,8,16,128]{3,2,1,0:T(8,128)S(1)} %copy-done.1, f32[32,81]{1,0:T(8,128)S(1)} %copy-done.2), custom_call_target="tpu_custom_call" | custom-call | tf_op jit(solution)/shard_map/snap/pallas_call | solution.py:243
  25.2 3.3 %basis.1 = f32[32,8,16,128]{3,2,1,0:T(8,128)} custom-call(f32[8,128]{1,0:T(8,128)S(1)} %get-tuple-element.7.t_ref, bf16[64,16384]{1,0:T(8,128)(2,1)S(1)} %get-tuple-element.8.s_ref), custom_call_target="tpu_custom_call" | custom-call | tf_op jit(solution)/shard_map/basis/pallas_call | solution.py:274
Async XLA Ops:
  0.0 0.9 %copy-start = (f32[3,8,16,128]{3,2,1,0:T(8,128)S(1)}, f32[3,8,16,128]{3,2,1,0:T(8,128)}, u32[]{:S(2)}) copy-start(f32[3,8,16,128]{3,2,1,0:T(8,128)} %f_ref.1) | copy-start | bytes 589828
  0.9 0.9 %copy-start.1 = (f32[3,8,16,128]{3,2,1,0:T(8,128)S(1)}, f32[3,8,16,128]{3,2,1,0:T(8,128)}, u32[]{:S(2)}) copy-start(f32[3,8,16,128]{3,2,1,0:T(8,128)} %a_ref.1) | copy-start | bytes 589828
  1.9 0.7 %copy-start.2 = (f32[32,81]{1,0:T(8,128)S(1)}, f32[32,81]{1,0:T(8,128)}, u32[]{:S(2)}) copy-start(f32[32,81]{1,0:T(8,128)} %w_ref.1) | copy-start | bytes 31108

commit v3 on v2

--- a/solution.py
+++ b/solution.py
@@ -11,8 +11,9 @@
 F32 = jnp.float32
 BF16 = jnp.bfloat16
 AXES = ("stream", "span", "depth")
+HBM = pl.BlockSpec(memory_space=pltpu.HBM)
 VMEM = pl.BlockSpec(memory_space=pltpu.VMEM)
-LIMIT = 48 * 1024 * 1024
+LIMIT = 56 * 1024 * 1024
 
 
 def split(value):
@@ -21,8 +22,8 @@
     return high, low
 
 
-def snap_kernel(sizes, f_ref, a_ref, w_ref, s_ref, t_ref, px, py, hy, hz, ysend, zsend, wv, gs, rhs, lhs, acc,
-                one, two, local, send, recv, send1, recv1, send2, recv2):
+def snap_kernel(sizes, f_ref, a_ref, w_ref, s_out, t_ref, s_ref, px, py, hy, hz, ysend, zsend, wv, gs, rhs, lhs, acc,
+                one, two, local, store, send, recv, send1, recv1, send2, recv2):
     n_s, n_y, n_z = sizes
     i_s, i_y, i_z = [lax.axis_index(name) for name in AXES]
     count = n_s * n_y
@@ -58,9 +59,30 @@
             load(ref.at[c], py.at[m * planes:(m + 1) * planes, 8:8 + rows])
         load(ref, px.at[3 * k:3 * k + 3, 2:planes + 2])
     load(w_ref, wv)
+    pl.semaphore_wait(barrier, count - 1 + n_z - 1)
+    copies = []
+
+    def push(src, dst, peer):
+        n = len(copies)
+        copy = pltpu.make_async_remote_copy(
+            src_ref=src, dst_ref=dst, send_sem=send.at[n], recv_sem=recv.at[n],
+            device_id=peer, device_id_type=MESH)
+        copy.start()
+        copies.append(copy)
+
+    def sides(name, size, mine):
+        return {name: lax.rem(mine + 1, size)}, {name: lax.rem(mine + size - 1, size)}
+
+    after_x, before_x = sides("stream", n_s, i_s)
+    after_y, before_y = sides("span", n_y, i_y)
+    after_z, before_z = sides("depth", n_z, i_z)
+    for k, ref in enumerate((f_ref, a_ref)):
+        push(ref.at[:, planes - 2:planes], px.at[3 * k:3 * k + 3, 0:2], after_x)
+    for k, ref in enumerate((f_ref, a_ref)):
+        push(ref.at[:, 0:2], px.at[3 * k:3 * k + 3, planes + 2:planes + 4], before_x)
+
     for copy in loads:
         copy.wait()
-
     flat = py.reshape(2 * half * tall, 128)
     for j in range(2):
         ysend[0, j] = flat[pl.ds(6 + rows + j, 2 * half, stride=tall), :]
@@ -80,31 +102,10 @@
         zsend[0, k] = last
         zsend[1, k] = first
 
-    pl.semaphore_wait(barrier, count - 1 + n_z - 1)
-    copies = []
-
-    def push(src, dst, peer):
-        n = len(copies)
-        copy = pltpu.make_async_remote_copy(
-            src_ref=src, dst_ref=dst, send_sem=send.at[n], recv_sem=recv.at[n],
-            device_id=peer, device_id_type=MESH)
-        copy.start()
-        copies.append(copy)
-
-    def sides(name, size, mine):
-        return {name: lax.rem(mine + 1, size)}, {name: lax.rem(mine + size - 1, size)}
-
-    after_x, before_x = sides("stream", n_s, i_s)
-    after_y, before_y = sides("span", n_y, i_y)
-    after_z, before_z = sides("depth", n_z, i_z)
     push(ysend.at[0], hy.at[0], after_y)
     push(ysend.at[1], hy.at[1], before_y)
     push(zsend.at[0], hz.at[0], after_z)
     push(zsend.at[1], hz.at[1], before_z)
-    for k, ref in enumerate((f_ref, a_ref)):
-        push(ref.at[:, planes - 2:planes], px.at[3 * k:3 * k + 3, 0:2], after_x)
-    for k, ref in enumerate((f_ref, a_ref)):
-        push(ref.at[:, 0:2], px.at[3 * k:3 * k + 3, planes + 2:planes + 4], before_x)
 
     row = lax.broadcasted_iota(jnp.int32, (81, 176), 0)
     col = lax.broadcasted_iota(jnp.int32, (81, 176), 1)
@@ -117,7 +118,7 @@
     lhs[32:64, :] = jnp.dot(w_low, pick, preferred_element_type=F32).astype(BF16)
     acc[...] = jnp.zeros_like(acc)
 
-    for copy in copies[:4]:
+    for copy in copies[4:8]:
         copy.wait()
     for j in range(2):
         flat[pl.ds(6 + j, 2 * half, stride=tall), :] = hy[0, j]
@@ -164,13 +165,23 @@
         s_ref[:, pl.ds(pl.multiple_of(x * cells, cells), cells)] = both
         acc[...] += lax.dot_general(both, both, (((1,), (1,)), ((), ())), preferred_element_type=F32)
 
+    def keep_plane(x):
+        part = pl.ds(x * cells, cells)
+        return pltpu.make_async_copy(s_ref.at[:, part], s_out.at[:, part], store.at[x])
+
     pl.loop(2, planes - 2)(plane)
-    for copy in copies[4:6]:
+    for x in range(2, planes - 2):
+        keep_plane(x).start()
+    for copy in copies[0:2]:
         copy.wait()
     pl.loop(0, 2)(plane)
-    for copy in copies[6:8]:
+    for x in range(2):
+        keep_plane(x).start()
+    for copy in copies[2:4]:
         copy.wait()
     pl.loop(planes - 2, planes)(plane)
+    for x in range(planes - 2, planes):
+        keep_plane(x).start()
 
     total = acc[0:32, :] + acc[32:64, :]
     gram = total[:, :32] + total[:, 32:]
@@ -193,6 +204,8 @@
 
     two[i_z] = exchange(one, me, count, plane_peer, send1, recv1)
     t_ref[...] = exchange(two, i_z, n_z, depth_peer, send2, recv2)
+    for x in range(planes):
+        keep_plane(x).wait()
 
 
 def factor(gram):
@@ -213,7 +226,15 @@
     return pltpu.roll(work, 96, 1) * lax.rsqrt(scale)
 
 
-def basis_kernel(cells, planes, t_ref, s_ref, o_ref, stage, sems):
+def basis_kernel(cells, planes, t_ref, s_in, o_ref, s_ref, stage, loads, sems):
+    width = s_in.shape[1] // planes
+
+    def fetch(x):
+        part = pl.ds(x * width, width)
+        return pltpu.make_async_copy(s_in.at[:, part], s_ref.at[:, part], loads.at[x])
+
+    for x in range(planes):
+        fetch(x).start()
     packed = t_ref[...] * (1.0 / cells)
     gram = jnp.concatenate([packed if q == 0 else pltpu.roll(packed, 128 - 32 * q, 1) for q in range(4)], axis=0)
     inverse = factor(gram)[:, :32]
@@ -224,7 +245,8 @@
     flat = stage.reshape(32 * planes * rows, 128)
     copies = []
     for x in range(planes):
-        wide = jnp.dot(left, s_ref[:, x * rows * 128:(x + 1) * rows * 128], preferred_element_type=F32)
+        fetch(x).wait()
+        wide = jnp.dot(left, s_ref[:, x * width:(x + 1) * width], preferred_element_type=F32)
         block = wide[:32] + wide[32:]
         for y in range(rows):
             flat[pl.ds(x * rows + y, 32, stride=planes * rows), :] = block[:, 128 * y:128 * y + 128]
@@ -245,9 +267,10 @@
         out_shape=(
             jax.ShapeDtypeStruct((64, planes * rows * depth), BF16),
             jax.ShapeDtypeStruct((8, 128), F32)),
-        in_specs=[pl.BlockSpec(memory_space=pltpu.HBM)] * 3,
-        out_specs=(VMEM,) * 2,
+        in_specs=[HBM] * 3,
+        out_specs=(HBM, VMEM),
         scratch_shapes=[
+            pltpu.VMEM((64, planes * rows * depth), BF16),
             pltpu.VMEM((6, planes + 4, rows, depth), F32),
             pltpu.VMEM((2 * half, rows + 16, depth), F32),
             pltpu.VMEM((2, 2, 2 * half, depth), F32),
@@ -262,6 +285,7 @@
             pltpu.VMEM((plane_count, 8, 128), F32),
             pltpu.VMEM((sizes[2], 8, 128), F32),
             pltpu.SemaphoreType.DMA((9,)),
+            pltpu.SemaphoreType.DMA((planes,)),
             pltpu.SemaphoreType.DMA((8,)),
             pltpu.SemaphoreType.DMA((8,)),
             pltpu.SemaphoreType.DMA((plane_count,)),
@@ -274,10 +298,12 @@
     return pl.pallas_call(
         functools.partial(basis_kernel, cells, planes),
         out_shape=jax.ShapeDtypeStruct((32, planes, rows, depth), F32),
-        in_specs=[VMEM] * 2,
-        out_specs=pl.BlockSpec(memory_space=pl.ANY),
+        in_specs=[VMEM, HBM],
+        out_specs=HBM,
         scratch_shapes=[
+            pltpu.VMEM((64, planes * rows * depth), BF16),
             pltpu.VMEM((32, planes * rows, depth), F32),
+            pltpu.SemaphoreType.DMA((planes,)),
             pltpu.SemaphoreType.DMA((planes,))],
         compiler_params=pltpu.CompilerParams(vmem_limit_bytes=LIMIT),
         name="basis",

time: 28.8 us -> 30.4 us (1.056)
  Pallas kernels: 26 us -> 30.2 us
  local copies, waits for them, and re-layouts: 2.57 us -> 0 us
    unnamed x6 -> x0, local copies, waits for them, and re-layouts: 2.57 us -> none
    pallas_call x1, Pallas kernels: 3.29 us -> 5.62 us  [body(): pl.pallas_call(functools.partial(basis_kernel, cells, planes), out_shape=...]
    pallas_call x1, Pallas kernels: 22.7 us -> 24.6 us  [body(): pl.pallas_call(functools.partial(snap_kernel, sizes), out_shape=(jax.Shap...]
where the time goes in v3:
time: 30.4 us; the launch traced here: 30.2 us
  Pallas kernels  30.2 us (99%)
    pallas_call x1, Pallas kernels, body(): pl.pallas_call(functools.partial(snap_kernel, sizes), out_shape=(jax.Shap...  24.6 us
    pallas_call x1, Pallas kernels, body(): pl.pallas_call(functools.partial(basis_kernel, cells, planes), out_shape=...  5.62 us

profile of v3, /device:TPU:0, one launch (start us, length us, event | category | flops | bytes accessed | tf_op | source)
XLA Modules:
  0.0 30.2 jit_solution(11147632737595114315)
XLA Ops:
  0.0 24.6 %snap.1 = (bf16[64,16384]{1,0:T(8,128)(2,1)}, f32[8,128]{1,0:T(8,128)}) custom-call(f32[3,8,16,128]{3,2,1,0:T(8,128)} %f_ref.1, f32[3,8,16,128]{3,2,1,0:T(8,128)} %a_ref.1, f32[32,81]{1,0:T(8,128)} %w_ref.1), custom_call_target="tpu_custom_call" | custom-call | tf_op jit(solution)/shard_map/snap/pallas_call | solution.py:265
  24.6 5.6 %basis.1 = f32[32,8,16,128]{3,2,1,0:T(8,128)} custom-call(f32[8,128]{1,0:T(8,128)} %get-tuple-element.7.t_ref, bf16[64,16384]{1,0:T(8,128)(2,1)} %get-tuple-element.8.s_in), custom_call_target="tpu_custom_call" | custom-call | tf_op jit(solution)/shard_map/basis/pallas_call | solution.py:298
